TPU v7x, 128 devices: a whole 4x4x4 slice. The times are simulated.
128 devices in a mesh: tm: 16 (over y, x_lo, core), space: 8 (over x_hi, z).
Axes of the slice: x: 4 (x_hi: 2, x_lo: 2; x = x_hi * 2 + x_lo), y: 4, z: 4, core: 2. Of those that a mesh axis runs over, the one named last changes fastest.
Arguments:
- snapshots: bfloat16 [16384, 65536], P('space', 'tm'), may hold values from -60 to 60
- basis: bfloat16 [16384, 64], P('space'), may hold values from -0.046875 to 0.046875
Outputs:
- reduced_rates: float32 [64, 65536], P(None, ('tm', 'space'))
- gram_quad: float32 [2080, 2080], P('tm', 'space')
- gram_side: float32 [65, 2145], replicated
- rhs: float32 [2145, 64], replicated
All inputs are finite; a program needn't handle non-finite values.
Results may differ from a plain program's by a relative error of at most 0.0003.
Values sent between devices are 32-bit elements; how exact they have to be, the bound alone decides.
A program may use at most 128 MiB of HBM per device.

v0:
```python
import jax
import jax.numpy as jnp
import numpy as np
from jax import lax
from jax.sharding import PartitionSpec as P


def padded_2(cells, sides, width):
    for axis, dim in sides:
        count = lax.axis_size(axis)
        ends = count - 1
        head = lax.slice_in_dim(cells, 0, width, axis=dim)
        tail = lax.slice_in_dim(cells, cells.shape[dim] - width, cells.shape[dim], axis=dim)
        cells = jnp.concatenate(
            [
                lax.ppermute(tail, axis, [(i, (i + 1) % count) for i in range(ends)]),
                cells,
                lax.ppermute(head, axis, [((i + 1) % count, i) for i in range(ends)]),
            ],
            axis=dim,
        )
    return cells


def rates_from(window, first, last):
    inner = window[:, 1:-1]
    left = jnp.where(first, 2.0 * inner[:, :1] - inner[:, 1:2], window[:, :1])
    right = jnp.where(last, 2.0 * inner[:, -1:] - inner[:, -2:-1], window[:, -1:])
    full = jnp.concatenate([left, inner, right], axis=1)
    return 0.5 * (full[:, 2:] - full[:, :-2])


def body(snapshots, basis):
    n_space = lax.axis_size("space")
    n_time = lax.axis_size("tm")
    space_idx = lax.axis_index("space")
    time_idx = lax.axis_index("tm")
    partial_proj = lax.dot_general(
        basis, snapshots, (((0,), (0,)), ((), ())), preferred_element_type=jnp.float32
    )
    slab = partial_proj.shape[1]
    width = slab // n_space
    summed = lax.psum(partial_proj, "space")
    padded = padded_2(summed, (("tm", 1),), 1)
    window = lax.dynamic_slice_in_dim(padded, space_idx * width, width + 2, 1)
    first = jnp.logical_and(time_idx == 0, space_idx == 0)
    last = jnp.logical_and(time_idx == n_time - 1, space_idx == n_space - 1)
    reduced = window[:, 1:-1]
    rates = rates_from(window, first, last)
    modes = reduced.shape[0]
    upper_i, upper_j = np.triu_indices(modes)
    quad = reduced[upper_i] * reduced[upper_j]
    side = jnp.concatenate([jnp.ones((1, width), jnp.float32), reduced], axis=0)
    feats = jnp.concatenate([quad, side], axis=0)
    scale = 1.0 / (slab * n_time)
    dims = (((1,), (1,)), ((), ()))
    high = lax.Precision.HIGHEST
    side_part = lax.dot_general(side, feats, dims, precision=high)
    rhs_part = lax.dot_general(feats, rates, dims, precision=high)
    side_total, rhs_total = lax.psum((side_part, rhs_part), ("tm", "space"))
    quad_part = lax.dot_general(quad, quad, dims, precision=high)
    row_block = lax.psum_scatter(quad_part, "tm", scatter_dimension=0, tiled=True)
    quad_block = lax.psum_scatter(row_block, "space", scatter_dimension=1, tiled=True)
    return (rates, quad_block * scale, side_total * scale, rhs_total * scale)


def solution(mesh):
    in_specs = (P("space", "tm"), P("space", None))
    out_specs = (P(None, ("tm", "space")), P("tm", "space"), P(), P())
    return jax.shard_map(body, mesh=mesh, in_specs=in_specs, out_specs=out_specs, check_vma=False)
```

profile of v0, /device:TPU:0, one launch (start us, length us, event | category | flops | bytes accessed | tf_op | source)
XLA Modules:
  0.0 658.8 jit_solution(12047642121125978018)
XLA Ops:
  7.2 0.0 copy-start
  7.2 0.0 copy-start.6
  7.2 0.0 copy-start.5
  7.2 0.0 all-reduce.9.cloned.1.call-start
  7.3 0.9 copy-done
  8.1 9.8 %fusion.7 = f32[64,4096]{1,0:T(8,128)} fusion(bf16[2048,64]{0,1:T(8,128)(2,1)S(1)} %copy-done, bf16[2048,4096]{1,0:T(8,128)(2,1)} %param.6), kind=kOutput, calls=%fused_computation.23 | convolution fusion | flops 1073741824 | bytes 18087936 | tf_op jit(solution)/shard_map/dot_general | solution.py:38
  17.9 0.0 all-reduce.9.cloned.1.call-update
  17.9 0.0 all-reduce.13.cloned.1.call-start
  18.0 0.0 copy-done.6
  18.0 0.0 copy-done.5
  18.0 90.4 %all-reduce.9.cloned.1.call-done = f32[64,4096]{1,0:T(8,128)} async-done(((f32[64,4096]{1,0:T(8,128)}), f32[64,4096]{1,0:T(8,128)}) %all-reduce.9.cloned.1.call-update) | async-done | bytes 1048592 | tf_op jit(solution)/shard_map/psum | solution.py:43
  108.4 0.8 fusion.6
  109.3 1.3 collective-permute-start
  110.6 1.3 collective-permute-start.1
  111.9 0.0 collective-permute-done
  111.9 2.6 collective-permute-done.1
  114.5 1.6 concatenate.17
  116.1 0.1 constant_dynamic-slice_fusion.1
  116.2 6.8 %gather_fusion = f32[2080,512]{1,0:T(8,128)} fusion(f32[64,512]{1,0:T(8,128)S(1)} %constant_dynamic-slice_fusion.1, s32[3072]{0:T(1024)S(1)} %pad_clamp_fusion.1), kind=kCustom, calls=%fused_computation | custom fusion | bytes 8528000 | tf_op jit(solution)/shard_map/gather | solution.py:52
  123.0 6.8 %gather_fusion.1 = f32[2080,512]{1,0:T(8,128)} fusion(f32[64,512]{1,0:T(8,128)S(1)} %constant_dynamic-slice_fusion.1, s32[3072]{0:T(1024)S(1)} %pad_clamp_fusion), kind=kCustom, calls=%fused_computation.1 | custom fusion | bytes 8528000 | tf_op jit(solution)/shard_map/gather | solution.py:52
  129.8 4.5 mul.41
  134.4 0.0 copy-start.2
  134.4 2.0 copy-done.2
  136.4 34.2 %fusion.8 = f32[2080,2080]{1,0:T(8,128)} fusion(f32[2080,512]{1,0:T(8,128)S(1)} %mul.41), kind=kOutput, calls=%fused_computation.24 | convolution fusion | flops 26581401600 | bytes 21565440 | tf_op jit(solution)/shard_map/dot_general | solution.py:61
  170.6 212.4 %fusion = f32[144,2080]{1,0:T(8,128)S(1)} fusion(f32[2080,2080]{1,0:T(8,128)} %fusion.8), kind=kCustom, calls=%all-reduce-scatter | all-reduce-scatter fusion | flops 4792321 | bytes 18504192
  383.0 2.4 collective-permute-start.2
  385.4 0.9 slice.57
  386.3 12.7 %concatenate.21 = f32[2145,512]{1,0:T(8,128)} concatenate(f32[2080,512]{1,0:T(8,128)} %copy-done.2, f32[1,512]{1,0:T(1,128)S(1)} %broadcast_in_dim.11, f32[64,512]{1,0:T(8,128)S(1)} %constant_dynamic-slice_fusion.1), dimensions={0} | concatenate | bytes 8785920 | tf_op jit(solution)/shard_map/concatenate | solution.py:54
  398.9 0.0 copy-start.3
  398.9 1.8 collective-permute-start.3
  400.7 0.1 dynamic-slice_select_fusion.1
  400.9 7.1 %fusion.1 = f32[65,2145]{1,0:T(8,128)} fusion(f32[2145,512]{1,0:T(8,128)} %concatenate.21, f32[64,512]{1,0:T(8,128)S(1)} %constant_dynamic-slice_fusion.1), kind=kOutput, calls=%fused_computation.5 | convolution fusion | flops 856627200 | bytes 5081732 | tf_op jit(solution)/shard_map/dot_general | solution.py:58
  407.9 0.0 copy-start.7
  407.9 0.0 copy-start.8
  407.9 0.1 fusion.4
  408.1 0.0 copy-done.3
  408.1 0.0 copy-start.4
  408.1 4.9 fusion.9
  413.0 0.0 all-reduce.13.cloned.1.call-update
  413.0 0.0 all-reduce.11.cloned.1.call-start
  413.0 0.0 copy-done.7
  413.0 0.6 dynamic-slice.13
  414.3 0.0 copy-done.8
  414.3 0.6 dynamic-slice.2
  415.5 0.0 collective-permute-done.3
  415.5 0.0 collective-permute-done.2
  415.6 0.0 copy-start.1
  415.6 12.0 %concatenate.22 = f32[354,2080]{1,0:T(8,128)} concatenate(f32[66,2080]{1,0:T(8,128)S(1)} %collective-permute-done.3, f32[144,2080]{1,0:T(8,128)} %collective-permute-done.2, f32[144,2080]{1,0:T(8,128)S(1)} %fusion), dimensions={0} | concatenate | bytes 5890560
  427.5 0.0 copy-done.4
  427.5 2.4 constant_dynamic-slice_fusion
  429.9 0.0 all-reduce.11.cloned.1.call-update
  430.0 129.8 %all-reduce.13.cloned.1.call-done = (f32[65,2145]{1,0:T(8,128)}, f32[2145,64]{0,1:T(8,128)}) async-done(((f32[65,2145]{1,0:T(8,128)}, f32[2145,64]{0,1:T(8,128)}), (f32[65,2145]{1,0:T(8,128)}, f32[2145,64]{0,1:T(8,128)})) %all-reduce.13.cloned.1.call-update) | async-done | bytes 1106836 | tf_op jit(solution)/shard_map/psum | solution.py:60
  559.8 1.9 broadcast_multiply_fusion.1
  561.7 1.9 broadcast_multiply_fusion
  563.6 86.9 %all-reduce.11.cloned.1.call-done = f32[130,2080]{1,0:T(8,128)} async-done(((f32[130,2080]{1,0:T(8,128)}), f32[130,2080]{1,0:T(8,128)}) %all-reduce.11.cloned.1.call-update) | async-done | bytes 1081616
  650.5 1.8 dynamic-slice_multiply_fusion
  652.2 0.0 copy-done.1
  (3 shorter events, 0.0 us)
Async XLA Ops:
  7.2 1.0 copy-start
  7.2 10.8 %copy-start.6 = (s32[2080]{0:T(1024)S(1)}, s32[2080]{0:T(1024)}, u32[]{:S(2)}) copy-start(s32[2080]{0:T(1024)} %constant.44) | copy-start | bytes 24964
  7.2 10.8 %copy-start.5 = (s32[2080]{0:T(1024)S(1)}, s32[2080]{0:T(1024)}, u32[]{:S(2)}) copy-start(s32[2080]{0:T(1024)} %constant.45) | copy-start | bytes 24964
  7.2 101.2 %all-reduce.9.cloned.1.call-start = ((), (), s32[]{:S(2)}) async-start(), calls=%async_computation | async-start | bytes 2097152 | tf_op jit(solution)/shard_map/psum | solution.py:43
  17.9 541.8 %all-reduce.13.cloned.1.call-start = ((), (), s32[]{:S(2)}) async-start(), calls=%async_computation.2 | async-start | bytes 2367488 | tf_op jit(solution)/shard_map/psum | solution.py:60
  109.3 2.6 collective-permute-start
  110.6 3.9 collective-permute-start.1
  134.4 2.0 copy-start.2
  383.0 32.5 %collective-permute-start.2 = (f32[144,2080]{1,0:T(8,128)S(1)}, f32[144,2080]{1,0:T(8,128)}, u32[]{:S(2)}, u32[]{:S(2)}) collective-permute-start(f32[144,2080]{1,0:T(8,128)S(1)} %fusion), channel_id=1, source_target_pairs={{0,8},{8,16},{16,24},{24,32},{32,40},{40,48},{48,56},{56,64},{64,7... | collective-permute-start | bytes 3594248
  398.9 9.2 %copy-start.3 = (f32[2145,512]{1,0:T(8,128)S(1)}, f32[2145,512]{1,0:T(8,128)}, u32[]{:S(2)}) copy-start(f32[2145,512]{1,0:T(8,128)} %concatenate.21) | copy-start | bytes 13178884
  398.9 16.6 %collective-permute-start.3 = (f32[66,2080]{1,0:T(8,128)}, f32[66,2080]{1,0:T(8,128)S(1)}, u32[]{:S(2)}, u32[]{:S(2)}) collective-permute-start(f32[66,2080]{1,0:T(8,128)} %slice.57), channel_id=1, source_target_pairs={{0,16},{8,24},{16,32},{24,40},{32,48},{40,56},{48,64},{56,72},{64,... | collective-permute-start | bytes 1647368
  407.9 5.1 copy-start.7
  407.9 6.4 copy-start.8
  408.1 19.4 %copy-start.4 = (f32[64,512]{1,0:T(8,128)}, f32[64,512]{1,0:T(8,128)S(1)}, u32[]{:S(2)}) copy-start(f32[64,512]{1,0:T(8,128)S(1)} %fusion.4) | copy-start | bytes 393220
  413.0 237.5 %all-reduce.11.cloned.1.call-start = ((), (), s32[]{:S(2)}) async-start(), calls=%async_computation.1 | async-start | bytes 2367488
  415.6 236.7 %copy-start.1 = (bf16[2048,64]{0,1:T(8,128)(2,1)S(1)}, bf16[2048,64]{0,1:T(8,128)(2,1)}, u32[]{:S(2)}) copy-start(bf16[2048,64]{0,1:T(8,128)(2,1)} %param.7) | copy-start | bytes 786436
Sparse Core Ops, SparseCore 0:
  18.1 90.3 all-reduce.8
  413.1 146.6 all-reduce.12
  562.5 87.9 all-reduce.10
where the time goes:
time: 660 us; the launch traced here: 659 us
  waiting for transfers between devices  310 us (47%)
  blocking collectives  212 us (32%)
  matrix products  55.9 us (8%)
  local copies, waits for them, and re-layouts  48.2 us (7%)
  between operations  15.3 us (2%)
  other arithmetic  10.4 us (2%)
  starting transfers between devices  6.87 us (1%)
    unnamed x1, blocking collectives  212 us
    psum x1, waiting for transfers between devices, body(): side_total, rhs_total = lax.psum((side_part, rhs_part), ('tm', 'space'))  130 us
    psum x1, waiting for transfers between devices, body(): summed = lax.psum(partial_proj, 'space')  90.4 us
    unnamed x6, waiting for transfers between devices  86.9 us
    dot_general x1, matrix products, body(): quad_part = lax.dot_general(quad, quad, dims, precision=high)  34.2 us
    unnamed x23, local copies, waits for them, and re-layouts  19.4 us
    gather x2, local copies, waits for them, and re-layouts, body(): quad = reduced[upper_i] * reduced[upper_j]  13.6 us
  transfers between devices with their start and end apart: 7, of which 4 were waited for; matrix products, arithmetic and copies ran while one was open for 7% of the time, Pallas kernels for 0%

commit v1 on v0

--- a/solution.py
+++ b/solution.py
@@ -40,7 +40,7 @@
     )
     slab = partial_proj.shape[1]
     width = slab // n_space
-    summed = lax.psum(partial_proj, "space")
+    summed = jnp.sum(lax.all_gather(partial_proj, "space"), axis=0)
     padded = padded_2(summed, (("tm", 1),), 1)
     window = lax.dynamic_slice_in_dim(padded, space_idx * width, width + 2, 1)
     first = jnp.logical_and(time_idx == 0, space_idx == 0)

time: 660 us -> 681 us (1.032)
  waiting for transfers between devices: 310 us -> 329 us
    all_gather x0 -> x1, waiting for transfers between devices: none -> 110 us  [body(): summed = jnp.sum(lax.all_gather(partial_proj, 'space'), axis=0)]
    psum x1 -> x0, waiting for transfers between devices: 90.4 us -> none  [body(): summed = lax.psum(partial_proj, 'space')]
where the time goes in v1:
time: 681 us; the launch traced here: 680 us
  waiting for transfers between devices  329 us (48%)
  blocking collectives  212 us (31%)
  matrix products  55.9 us (8%)
  local copies, waits for them, and re-layouts  46.5 us (7%)
  between operations  15.3 us (2%)
  other arithmetic  14.4 us (2%)
  starting transfers between devices  6.91 us (1%)
    unnamed x1, blocking collectives  212 us
    psum x1, waiting for transfers between devices, body(): side_total, rhs_total = lax.psum((side_part, rhs_part), ('tm', 'space'))  129 us
    all_gather x1, waiting for transfers between devices, body(): summed = jnp.sum(lax.all_gather(partial_proj, 'space'), axis=0)  110 us
    unnamed x6, waiting for transfers between devices  86.9 us
    dot_general x1, matrix products, body(): quad_part = lax.dot_general(quad, quad, dims, precision=high)  34.2 us
    unnamed x23, local copies, waits for them, and re-layouts  19.4 us
    gather x2, local copies, waits for them, and re-layouts, body(): quad = reduced[upper_i] * reduced[upper_j]  13.6 us
  transfers between devices with their start and end apart: 7, of which 4 were waited for; matrix products, arithmetic and copies ran while one was open for 7% of the time, Pallas kernels for 0%

profile of v1, /device:TPU:0, one launch (start us, length us, event | category | flops | bytes accessed | tf_op | source)
XLA Modules:
  0.0 680.0 jit_solution(14268050465593376441)
XLA Ops:
  7.2 0.0 copy-start
  7.2 0.0 copy-start.6
  7.2 0.0 copy-start.5
  7.2 0.0 all-gather.3.cloned.1.call-start
  7.3 0.9 copy-done
  8.1 9.9 %fusion.7 = f32[64,4096]{1,0:T(8,128)} fusion(bf16[2048,64]{0,1:T(8,128)(2,1)S(1)} %copy-done, bf16[2048,4096]{1,0:T(8,128)(2,1)} %param.6), kind=kOutput, calls=%fused_computation.23 | convolution fusion | flops 1073741824 | bytes 18087936 | tf_op jit(solution)/shard_map/dot_general | solution.py:38
  18.0 0.0 all-gather.3.cloned.1.call-update
  18.0 0.0 all-reduce.10.cloned.1.call-start
  18.1 0.0 copy-done.6
  18.1 0.0 copy-done.5
  18.1 109.8 %all-gather.3.cloned.1.call-done = f32[512,4096]{1,0:T(8,128)} async-done(((f32[64,4096]{1,0:T(8,128)}), f32[512,4096]{1,0:T(8,128)}) %all-gather.3.cloned.1.call-update) | async-done | bytes 8388624 | tf_op jit(solution)/shard_map/all_gather | solution.py:43
  127.9 4.0 reduce_sum.9
  131.8 0.1 fusion.6
  131.9 1.3 collective-permute-start
  133.3 1.3 collective-permute-start.1
  134.6 0.0 collective-permute-done
  134.6 2.6 collective-permute-done.1
  137.1 0.6 concatenate.17
  137.8 0.1 constant_dynamic-slice_fusion.1
  137.9 6.8 %gather_fusion = f32[2080,512]{1,0:T(8,128)} fusion(f32[64,512]{1,0:T(8,128)S(1)} %constant_dynamic-slice_fusion.1, s32[3072]{0:T(1024)S(1)} %pad_clamp_fusion.1), kind=kCustom, calls=%fused_computation | custom fusion | bytes 8528000 | tf_op jit(solution)/shard_map/gather | solution.py:52
  144.7 6.8 %gather_fusion.1 = f32[2080,512]{1,0:T(8,128)} fusion(f32[64,512]{1,0:T(8,128)S(1)} %constant_dynamic-slice_fusion.1, s32[3072]{0:T(1024)S(1)} %pad_clamp_fusion), kind=kCustom, calls=%fused_computation.1 | custom fusion | bytes 8528000 | tf_op jit(solution)/shard_map/gather | solution.py:52
  151.5 4.5 mul.41
  156.1 0.0 copy-start.2
  156.1 2.0 copy-done.2
  158.1 34.2 %fusion.8 = f32[2080,2080]{1,0:T(8,128)} fusion(f32[2080,512]{1,0:T(8,128)S(1)} %mul.41), kind=kOutput, calls=%fused_computation.24 | convolution fusion | flops 26581401600 | bytes 21565440 | tf_op jit(solution)/shard_map/dot_general | solution.py:61
  192.3 212.4 %fusion = f32[144,2080]{1,0:T(8,128)S(1)} fusion(f32[2080,2080]{1,0:T(8,128)} %fusion.8), kind=kCustom, calls=%all-reduce-scatter | all-reduce-scatter fusion | flops 4792321 | bytes 18504192
  404.7 2.4 collective-permute-start.2
  407.1 0.9 slice.57
  407.9 12.7 %concatenate.21 = f32[2145,512]{1,0:T(8,128)} concatenate(f32[2080,512]{1,0:T(8,128)} %copy-done.2, f32[1,512]{1,0:T(1,128)S(1)} %broadcast_in_dim.11, f32[64,512]{1,0:T(8,128)S(1)} %constant_dynamic-slice_fusion.1), dimensions={0} | concatenate | bytes 8785920 | tf_op jit(solution)/shard_map/concatenate | solution.py:54
  420.6 0.0 copy-start.3
  420.6 1.8 collective-permute-start.3
  422.4 0.1 dynamic-slice_select_fusion.1
  422.5 7.1 %fusion.1 = f32[65,2145]{1,0:T(8,128)} fusion(f32[2145,512]{1,0:T(8,128)} %concatenate.21, f32[64,512]{1,0:T(8,128)S(1)} %constant_dynamic-slice_fusion.1), kind=kOutput, calls=%fused_computation.5 | convolution fusion | flops 856627200 | bytes 5081732 | tf_op jit(solution)/shard_map/dot_general | solution.py:58
  429.6 0.0 copy-start.7
  429.6 0.0 copy-start.8
  429.6 0.1 fusion.4
  429.8 0.0 copy-done.3
  429.8 0.0 copy-start.4
  429.8 4.9 fusion.9
  434.6 0.0 all-reduce.10.cloned.1.call-update
  434.7 0.0 all-reduce.8.cloned.1.call-start
  434.7 0.0 copy-done.7
  434.7 0.6 dynamic-slice.13
  436.0 0.0 copy-done.8
  436.0 0.6 dynamic-slice.2
  437.2 0.0 collective-permute-done.3
  437.2 0.0 collective-permute-done.2
  437.2 0.0 copy-start.1
  437.2 12.0 %concatenate.22 = f32[354,2080]{1,0:T(8,128)} concatenate(f32[66,2080]{1,0:T(8,128)S(1)} %collective-permute-done.3, f32[144,2080]{1,0:T(8,128)} %collective-permute-done.2, f32[144,2080]{1,0:T(8,128)S(1)} %fusion), dimensions={0} | concatenate | bytes 5890560
  449.2 0.0 copy-done.4
  449.2 2.4 constant_dynamic-slice_fusion
  451.6 0.0 all-reduce.8.cloned.1.call-update
  451.7 129.3 %all-reduce.10.cloned.1.call-done = (f32[65,2145]{1,0:T(8,128)}, f32[2145,64]{0,1:T(8,128)}) async-done(((f32[65,2145]{1,0:T(8,128)}, f32[2145,64]{0,1:T(8,128)}), (f32[65,2145]{1,0:T(8,128)}, f32[2145,64]{0,1:T(8,128)})) %all-reduce.10.cloned.1.call-update) | async-done | bytes 1106836 | tf_op jit(solution)/shard_map/psum | solution.py:60
  581.0 1.9 broadcast_multiply_fusion.1
  582.9 1.9 broadcast_multiply_fusion
  584.8 86.9 %all-reduce.8.cloned.1.call-done = f32[130,2080]{1,0:T(8,128)} async-done(((f32[130,2080]{1,0:T(8,128)}), f32[130,2080]{1,0:T(8,128)}) %all-reduce.8.cloned.1.call-update) | async-done | bytes 1081616
  671.7 1.8 dynamic-slice_multiply_fusion
  673.4 0.0 copy-done.1
  (3 shorter events, 0.0 us)
Async XLA Ops:
  7.2 1.0 copy-start
  7.2 10.9 %copy-start.6 = (s32[2080]{0:T(1024)S(1)}, s32[2080]{0:T(1024)}, u32[]{:S(2)}) copy-start(s32[2080]{0:T(1024)} %constant.46) | copy-start | bytes 24964
  7.2 10.9 %copy-start.5 = (s32[2080]{0:T(1024)S(1)}, s32[2080]{0:T(1024)}, u32[]{:S(2)}) copy-start(s32[2080]{0:T(1024)} %constant.47) | copy-start | bytes 24964
  7.2 120.7 %all-gather.3.cloned.1.call-start = ((), (), s32[]{:S(2)}) async-start(), calls=%async_computation | async-start | bytes 9437184 | tf_op jit(solution)/shard_map/all_gather | solution.py:43
  18.0 563.0 %all-reduce.10.cloned.1.call-start = ((), (), s32[]{:S(2)}) async-start(), calls=%async_computation.2 | async-start | bytes 2367488 | tf_op jit(solution)/shard_map/psum | solution.py:60
  131.9 2.6 collective-permute-start
  133.3 3.9 collective-permute-start.1
  156.1 2.0 copy-start.2
  404.7 32.5 %collective-permute-start.2 = (f32[144,2080]{1,0:T(8,128)S(1)}, f32[144,2080]{1,0:T(8,128)}, u32[]{:S(2)}, u32[]{:S(2)}) collective-permute-start(f32[144,2080]{1,0:T(8,128)S(1)} %fusion), channel_id=1, source_target_pairs={{0,8},{8,16},{16,24},{24,32},{32,40},{40,48},{48,56},{56,64},{64,7... | collective-permute-start | bytes 3594248
  420.6 9.2 %copy-start.3 = (f32[2145,512]{1,0:T(8,128)S(1)}, f32[2145,512]{1,0:T(8,128)}, u32[]{:S(2)}) copy-start(f32[2145,512]{1,0:T(8,128)} %concatenate.21) | copy-start | bytes 13178884
  420.6 16.6 %collective-permute-start.3 = (f32[66,2080]{1,0:T(8,128)}, f32[66,2080]{1,0:T(8,128)S(1)}, u32[]{:S(2)}, u32[]{:S(2)}) collective-permute-start(f32[66,2080]{1,0:T(8,128)} %slice.57), channel_id=1, source_target_pairs={{0,16},{8,24},{16,32},{24,40},{32,48},{40,56},{48,64},{56,72},{64,... | collective-permute-start | bytes 1647368
  429.6 5.1 copy-start.7
  429.6 6.4 copy-start.8
  429.8 19.4 %copy-start.4 = (f32[64,512]{1,0:T(8,128)}, f32[64,512]{1,0:T(8,128)S(1)}, u32[]{:S(2)}) copy-start(f32[64,512]{1,0:T(8,128)S(1)} %fusion.4) | copy-start | bytes 393220
  434.7 237.0 %all-reduce.8.cloned.1.call-start = ((), (), s32[]{:S(2)}) async-start(), calls=%async_computation.1 | async-start | bytes 2367488
  437.2 236.2 %copy-start.1 = (bf16[2048,64]{0,1:T(8,128)(2,1)S(1)}, bf16[2048,64]{0,1:T(8,128)(2,1)}, u32[]{:S(2)}) copy-start(bf16[2048,64]{0,1:T(8,128)(2,1)} %param.7) | copy-start | bytes 786436
Sparse Core Ops, SparseCore 0:
  18.1 109.7 all-gather.2
  434.8 146.1 all-reduce.9
  583.7 87.9 all-reduce.7
